TPU v7x, 32 devices: a whole 2x2x4 slice. The times are simulated.
32 devices in a mesh: grp: 8 (over y, x, core), sub: 4 (over z).
Axes of the slice: x: 2, y: 2, z: 4, core: 2. Of those that a mesh axis runs over, the one named last changes fastest.
Arguments:
- eigvecs: bfloat16 [8, 4, 32, 3072], P('grp', 'sub'), may hold values from -1 to 1
- local_blocks: bfloat16 [8, 4, 32, 7, 4096], P('grp', 'sub'), may hold values from -0.25 to 0.25
- local_cols: int32 [8, 4, 32, 7], P('grp', 'sub'), may hold values from 0 to 31
- margin_rows: int32 [8, 4, 4, 256], P('grp', 'sub'), may hold values from 0 to 511
- margin_lens: int32 [8, 4, 4], P('grp', 'sub'), may hold values from 1 to 256
- peer_blocks: bfloat16 [8, 4, 4, 4, 4096], P('grp', 'sub'), may hold values from -0.75 to 0.75
- peer_rowblocks: int32 [8, 4, 4, 4], P('grp', 'sub'), may hold values from 0 to 31
- cross_blocks: bfloat16 [8, 4, 2, 2, 4096], P('grp', 'sub'), may hold values from -0.75 to 0.75
- cross_rowblocks: int32 [8, 4, 2, 2], P('grp', 'sub'), may hold values from 0 to 31
Outputs:
- group_matrix: float32 [8, 192, 192], P('grp')
- cross_rows: float32 [8, 4, 2, 48, 48], P('grp', 'sub')
All inputs are finite; a program needn't handle non-finite values.
Results may differ from a plain program's by a relative error of at most 0.0029.
Values may be sent and summed in bfloat16 or wider, within the bound.
A program may use at most 64 MiB of HBM per device.

v0:
```python
import functools

import jax
import jax.numpy as jnp
from jax import lax
from jax.experimental import pallas as pl
from jax.experimental.pallas import tpu as pltpu
from jax.sharding import PartitionSpec as P

K = 48
BND = 512
CAP = 256
FACE = 128
LANES = 128
HALF = 64
MESH = pl.DeviceIdType.MESH
F32 = jnp.float32
BF16 = jnp.bfloat16


def dot_t(a, b):
    return lax.dot_general(a, b, (((1,), (1,)), ((), ())), preferred_element_type=F32)


def dot(a, b):
    return lax.dot_general(a, b, (((1,), (0,)), ((), ())), preferred_element_type=F32)


def kernel(
    subs,
    grps,
    z_hbm,
    lb_hbm,
    pb_hbm,
    cb_hbm,
    cols_hbm,
    rows_hbm,
    lens_hbm,
    prow_hbm,
    crow_hbm,
    out_ref,
    cross_ref,
    cols,
    rows_ref,
    lens,
    prow,
    crow,
    z_v,
    lb_v,
    pb_v,
    cb_v,
    zf,
    zi,
    lf,
    pf,
    cf,
    zz,
    zd,
    zpair,
    take_s,
    take_r,
    mix_s,
    mix_r,
    face,
    a_all,
    d_all,
    got,
    gath,
    in_sem,
    lb_sem,
    ts_sem,
    tr_sem,
    ls_sem,
    lr_sem,
    fs_sem,
    fr_sem,
    rs_sem,
    rr_sem,
):
    me = lax.axis_index("sub")
    g = lax.axis_index("grp")
    nblk = z_v.shape[0]
    nnz = lb_v.shape[0]
    pairs = nblk // 2
    step = nblk + 8
    ncb = CAP // 64
    nfb = FACE // 64

    barrier = pltpu.get_barrier_semaphore()
    for d in range(1, subs):
        pl.semaphore_signal(
            barrier, inc=1, device_id={"sub": lax.rem(me + d, subs)}, device_id_type=MESH
        )

    @pl.when(g > 0)
    def _():
        pl.semaphore_signal(barrier, inc=1, device_id={"grp": g - 1}, device_id_type=MESH)

    @pl.when(g < grps - 1)
    def _():
        pl.semaphore_signal(barrier, inc=1, device_id={"grp": g + 1}, device_id_type=MESH)

    z_in = pltpu.make_async_copy(z_hbm, z_v, in_sem.at[0])
    z_in.start()
    pb_in = pltpu.make_async_copy(pb_hbm, pb_v, in_sem.at[1])
    pb_in.start()
    cb_in = pltpu.make_async_copy(cb_hbm, cb_v, in_sem.at[2])
    cb_in.start()
    small_in = [
        pltpu.make_async_copy(a, b, in_sem.at[3 + i])
        for i, (a, b) in enumerate(
            [
                (prow_hbm, prow),
                (lens_hbm, lens),
                (rows_hbm, rows_ref),
                (cols_hbm, cols),
                (crow_hbm, crow),
            ]
        )
    ]
    for c in small_in:
        c.start()
    lb_in = [pltpu.make_async_copy(lb_hbm.at[t], lb_v.at[t], lb_sem.at[t]) for t in range(nnz)]
    for t in range(nnz):
        lb_in[t].start()

    lane = lax.broadcasted_iota(jnp.int32, (1, LANES), 1)
    lo = lane < HALF

    z_in.wait()
    for q in range(K // 2):
        zf[q * nblk : (q + 1) * nblk, :] = z_v[:, q * LANES : (q + 1) * LANES].astype(F32)

    def z_body(i, carry):
        for s in range(2):
            r = i * 2 + s
            v = zf[pl.ds(r, K // 2, stride=nblk), :]
            w = pltpu.roll(v, HALF, 1)
            zi[pl.ds(r * K, K // 2, stride=2), :] = jnp.where(lo, v, w)
            zi[pl.ds(r * K + 1, K // 2, stride=2), :] = jnp.where(lo, w, v)
        a = zi[pl.ds(i * 2 * K, K), :]
        b = zi[pl.ds(i * 2 * K + K, K), :]
        zz[i * 2] = a.astype(BF16)
        zz[i * 2 + 1] = b.astype(BF16)
        zpair[i] = jnp.where(lo, a, b).astype(BF16)
        return carry

    lax.fori_loop(0, pairs, z_body, 0, unroll=4)

    src = lax.broadcasted_iota(jnp.int32, (LANES, LANES), 0)
    dst = lax.broadcasted_iota(jnp.int32, (LANES, LANES), 1) % HALF
    want = jnp.where(dst < 32, dst * 2, (dst - 32) * 2 + 1)
    sel = jnp.where(src == want, 1.0, 0.0).astype(BF16)

    def d_body(i, carry):
        both = jnp.concatenate([zz[i * 2], zz[i * 2 + 1]], axis=0)
        moved = dot(both, sel)
        a, b = moved[:K], moved[K:]
        zd[i * 2] = a.astype(BF16)
        zd[i * 2 + 1] = b.astype(BF16)
        d_all[:, pl.ds(pl.multiple_of(i * LANES, LANES), LANES)] = jnp.where(lo, a, b).astype(BF16)
        return carry

    lax.fori_loop(0, pairs, d_body, 0, unroll=8)

    pb_in.wait()
    cb_in.wait()
    for c in small_in:
        c.wait()

    def unfold(x0, x1):
        e = jnp.where(lo, x0, pltpu.roll(x1, HALF, 1))
        o = jnp.where(lo, pltpu.roll(x0, HALF, 1), x1)
        return jnp.concatenate([e, o], axis=0).astype(BF16)

    def mix(x0, x1, r0, r1):
        both = jnp.concatenate([zd[r0], zd[r1]], axis=0)[:, :HALF]
        m = dot(both, unfold(x0, x1))
        return jnp.where(lo, m[:K], m[K:]).astype(BF16)

    def p_body(p, carry):
        for m in range(32):
            pf[m * 8 : m * 8 + ncb, :] = pb_v[p, :, m * LANES : (m + 1) * LANES].astype(F32)
        parts = []
        for c in range(0, ncb, 2):
            x0 = pf[pl.ds(c, 32, stride=8), :]
            x1 = pf[pl.ds(c + 1, 32, stride=8), :]
            parts.append(mix(x0, x1, prow[p, c], prow[p, c + 1]))
        mixed = jnp.concatenate(parts, axis=1)
        slots = lax.broadcasted_iota(jnp.int32, (1, CAP), 1)
        limit = jnp.where(p == me, 0, lens[0, p])
        take_s[p] = jnp.where(slots < limit, rows_ref[pl.ds(p, 1), :], -1)
        mix_s[p] = mixed
        return carry

    lax.fori_loop(0, subs, p_body, 0)
    take_r[me] = jnp.full((1, CAP), -1, jnp.int32)
    mix_r[me] = jnp.zeros((K, CAP), BF16)

    waits = subs - 1 + (g > 0).astype(jnp.int32) + (g < grps - 1).astype(jnp.int32)
    pl.semaphore_wait(barrier, waits)

    def take_copy(mine, theirs, peer):
        return pltpu.make_async_remote_copy(
            src_ref=take_s.at[mine],
            dst_ref=take_r.at[theirs],
            send_sem=ts_sem.at[mine],
            recv_sem=tr_sem.at[theirs],
            device_id={"sub": peer},
            device_id_type=MESH,
        )

    def mix_copy(mine, theirs, peer):
        return pltpu.make_async_remote_copy(
            src_ref=mix_s.at[mine],
            dst_ref=mix_r.at[theirs],
            send_sem=ls_sem.at[mine],
            recv_sem=lr_sem.at[theirs],
            device_id={"sub": peer},
            device_id_type=MESH,
        )

    peers = [lax.rem(me + d, subs) for d in range(1, subs)]
    for peer in peers:
        take_copy(peer, me, peer).start()
    for peer in peers:
        mix_copy(peer, me, peer).start()

    def face_copy(side, target):
        return pltpu.make_async_remote_copy(
            src_ref=zpair.at[BND // LANES + 1 - side],
            dst_ref=face.at[side],
            send_sem=fs_sem.at[side],
            recv_sem=fr_sem.at[side],
            device_id={"grp": target},
            device_id_type=MESH,
        )

    @pl.when(g < grps - 1)
    def _():
        face_copy(0, g + 1).start()

    @pl.when(g > 0)
    def _():
        face_copy(1, g - 1).start()


    for t in range(nnz):
        lb_in[t].wait()

    def l_body(t, carry):
        for m in range(32):
            lf[pl.ds((t * 32 + m) * step, nblk), :] = lb_v[
                t, :, m * LANES : (m + 1) * LANES
            ].astype(F32)
        return carry

    lax.fori_loop(0, nnz, l_body, 0)

    zero = jnp.zeros((32, LANES), F32)

    def own_part(r):
        weights, moving = [], []
        for t in range(0, nnz, 2):
            x0 = lf[pl.ds(t * 32 * step + r, 32, stride=step), :]
            if t + 1 < nnz:
                x1 = lf[pl.ds((t + 1) * 32 * step + r, 32, stride=step), :]
                vec = jnp.where(lo, zz[cols[t, 0, r]], zz[cols[t + 1, 0, r]])
            else:
                x1 = zero
                vec = zz[cols[t, 0, r]]
            weights.append(unfold(x0, x1))
            moving.append(vec)
        return dot_t(jnp.concatenate(moving, axis=1), jnp.concatenate(weights, axis=1))

    def r_body(i, carry):
        a = own_part(i * 2)
        b = own_part(i * 2 + 1)
        a_all[:, pl.ds(pl.multiple_of(i * LANES, LANES), LANES)] = jnp.concatenate(
            [a, b], axis=1
        ).astype(BF16)
        return carry

    lax.fori_loop(0, pairs, r_body, 0, unroll=8)
    own = dot_t(a_all[...], d_all[...])

    layer = jnp.concatenate([zpair[h] for h in range(BND // LANES)], axis=1)
    for peer in peers:
        take_copy(peer, peer, peer).wait_recv()

    def g_body(p, carry):
        cells = lax.broadcasted_iota(jnp.int32, (BND, CAP), 0)
        hot = jnp.where(cells == take_r[p], 1.0, 0.0).astype(BF16)
        got[p] = dot(layer, hot).astype(BF16)
        return carry

    lax.fori_loop(0, subs, g_body, 0)

    for peer in peers:
        mix_copy(peer, peer, peer).wait_recv()
    blocks = []
    for p in range(subs):
        blocks.append(dot_t(got[p], mix_r[p]) + jnp.where(p == me, 1.0, 0.0) * own)
    gath[me] = jnp.concatenate(blocks, axis=1).astype(BF16)

    def row_copy(slot, peer):
        return pltpu.make_async_remote_copy(
            src_ref=gath.at[slot],
            dst_ref=gath.at[slot],
            send_sem=rs_sem.at[peer],
            recv_sem=rr_sem.at[slot],
            device_id={"sub": peer},
            device_id_type=MESH,
        )

    for peer in peers:
        row_copy(me, peer).start()

    @pl.when(g > 0)
    def _():
        face_copy(0, g + 1).wait_recv()

    @pl.when(g == 0)
    def _():
        face[0] = jnp.zeros((K, LANES), BF16)

    @pl.when(g < grps - 1)
    def _():
        face_copy(1, g - 1).wait_recv()

    @pl.when(g == grps - 1)
    def _():
        face[1] = jnp.zeros((K, LANES), BF16)

    for q in range(2):
        for m in range(32):
            cf[q * 256 + m * 8 : q * 256 + m * 8 + nfb, :] = cb_v[
                q, :, m * LANES : (m + 1) * LANES
            ].astype(F32)
        x0 = cf[pl.ds(q * 256, 32, stride=8), :]
        x1 = cf[pl.ds(q * 256 + 1, 32, stride=8), :]
        mixed = mix(x0, x1, crow[q, 0], crow[q, 1])
        cross_ref[q] = dot_t(mixed, face[q])

    @pl.when(g < grps - 1)
    def _():
        face_copy(0, g + 1).wait_send()

    @pl.when(g > 0)
    def _():
        face_copy(1, g - 1).wait_send()

    for peer in peers:
        take_copy(peer, me, peer).wait_send()
        mix_copy(peer, me, peer).wait_send()
    for peer in peers:
        row_copy(peer, peer).wait_recv()
    side = subs * K
    unit = jnp.where(
        lax.broadcasted_iota(jnp.int32, (side, side), 0)
        == lax.broadcasted_iota(jnp.int32, (side, side), 1),
        1.0,
        0.0,
    ).astype(BF16)
    out_ref[...] = dot_t(unit, jnp.concatenate([gath[p] for p in range(subs)], axis=0))
    for peer in peers:
        row_copy(me, peer).wait_send()


def per_device(
    eigvecs,
    local_blocks,
    local_cols,
    margin_rows,
    margin_lens,
    peer_blocks,
    peer_rowblocks,
    cross_blocks,
    cross_rowblocks,
):
    subs = lax.axis_size("sub")
    grps = lax.axis_size("grp")
    z = eigvecs[0, 0]
    lb = jnp.transpose(local_blocks[0, 0], (1, 0, 2))
    cols = jnp.transpose(local_cols[0], (2, 0, 1))
    nblk = z.shape[0]
    nnz = lb.shape[0]
    pb = peer_blocks[0, 0]
    cb = cross_blocks[0, 0]
    vmem = pl.BlockSpec(memory_space=pltpu.VMEM)
    hbm = pl.BlockSpec(memory_space=pltpu.HBM)
    dma = pltpu.SemaphoreType.DMA
    group_matrix, crossed = pl.pallas_call(
        functools.partial(kernel, subs, grps),
        out_shape=(
            pltpu.VMEM((subs * K, subs * K), F32),
            pltpu.VMEM((2, K, K), F32),
        ),
        in_specs=[hbm] * 9,
        out_specs=(vmem, vmem),
        scratch_shapes=[
            pltpu.SMEM(cols.shape, jnp.int32),
            pltpu.VMEM(margin_rows.shape[2:], jnp.int32),
            pltpu.SMEM((1, subs), jnp.int32),
            pltpu.SMEM(peer_rowblocks.shape[2:], jnp.int32),
            pltpu.SMEM(cross_rowblocks.shape[2:], jnp.int32),
            pltpu.VMEM(z.shape, BF16),
            pltpu.VMEM(lb.shape, BF16),
            pltpu.VMEM(pb.shape, BF16),
            pltpu.VMEM(cb.shape, BF16),
            pltpu.VMEM((K // 2 * nblk, LANES), F32),
            pltpu.VMEM((nblk * K, LANES), F32),
            pltpu.VMEM((nnz * 32 * (nblk + 8), LANES), F32),
            pltpu.VMEM((256, LANES), F32),
            pltpu.VMEM((512, LANES), F32),
            pltpu.VMEM((nblk, K, LANES), BF16),
            pltpu.VMEM((nblk, K, LANES), BF16),
            pltpu.VMEM((nblk // 2, K, LANES), BF16),
            pltpu.VMEM((subs, 1, CAP), jnp.int32),
            pltpu.VMEM((subs, 1, CAP), jnp.int32),
            pltpu.VMEM((subs, K, CAP), BF16),
            pltpu.VMEM((subs, K, CAP), BF16),
            pltpu.VMEM((2, K, LANES), BF16),
            pltpu.VMEM((K, nblk * HALF), BF16),
            pltpu.VMEM((K, nblk * HALF), BF16),
            pltpu.VMEM((subs, K, CAP), BF16),
            pltpu.VMEM((subs, K, subs * K), BF16),
            dma((8,)),
            dma((nnz,)),
            dma((subs,)),
            dma((subs,)),
            dma((subs,)),
            dma((subs,)),
            dma((2,)),
            dma((2,)),
            dma((subs,)),
            dma((subs,)),
        ],
        compiler_params=pltpu.CompilerParams(
            collective_id=0, has_side_effects=True, vmem_limit_bytes=48 * 1024 * 1024
        ),
    )(
        *[
            pltpu.with_memory_space_constraint(x, pltpu.HBM)
            for x in (
                z,
                lb,
                pb,
                cb,
                cols,
                margin_rows[0, 0],
                margin_lens[0],
                peer_rowblocks[0, 0],
                cross_rowblocks[0, 0],
            )
        ]
    )
    return group_matrix[None], crossed[None, None]


def solution(mesh):
    return jax.shard_map(
        per_device,
        mesh=mesh,
        in_specs=(
            P("grp", "sub", None, None),
            P("grp", "sub", None, None, None),
            P("grp", "sub", None, None),
            P("grp", "sub", None, None),
            P("grp", "sub", None),
            P("grp", "sub", None, None, None),
            P("grp", "sub", None, None),
            P("grp", "sub", None, None, None),
            P("grp", "sub", None, None),
        ),
        out_specs=(P("grp", None, None), P("grp", "sub", None, None, None)),
        check_vma=False,
    )
```

profile of v0, /device:TPU:0, one launch (start us, length us, event | category | flops | bytes accessed | tf_op | source)
XLA Modules:
  0.0 15.9 jit_solution(3314752859205018052)
XLA Ops:
  0.6 14.0 %shard_map.104 = (f32[192,192]{1,0:T(8,128)S(1)}, f32[2,48,48]{2,1,0:T(8,128)S(1)}) custom-call(bf16[32,3072]{1,0:T(8,128)(2,1)} %bitcast.18, bf16[7,32,4096]{2,1,0:T(8,128)(2,1)} %bitcast.17, bf16[4,4,4096]{2,1,0:T(4,128)(2,1)} %bitcast.19, bf16[2,2,4096]{2,1,0:T(2,128)(2,1)} %bitcast.20, s32[7,1,32]{2,1,0:T(1,128)} %bitcast.22, s32[4,256]{1,0:T(4,128)} %bitcast.21, ...), custom_call_target="tpu_custom_call" | custom-call | tf_op jit(solution)/shard_map/pallas_call | solution.py:393
  14.6 0.7 %copy.13 = f32[1,192,192]{2,1,0:T(8,128)} copy(f32[1,192,192]{2,1,0:T(8,128)S(1)} %bitcast.15) | data formatting | bytes 294912
  15.3 0.6 %copy.14 = f32[1,1,2,48,48]{4,3,2,1,0:T(8,128)} copy(f32[1,1,2,48,48]{4,3,2,1,0:T(8,128)S(1)} %bitcast.16) | data formatting | bytes 36864
where the time goes:
time: 16.1 us; the launch traced here: 15.9 us
  Pallas kernels  14 us (87%)
  local copies, waits for them, and re-layouts  1.3 us (8%)
  between operations  0.64 us (4%)
    pallas_call x1, Pallas kernels, per_device(): pl.pallas_call(functools.partial(kernel, subs, grps), out_shape=(pltpu.VM...  14 us
    unnamed x2, local copies, waits for them, and re-layouts  1.3 us

commit v1 on v0

--- a/solution.py
+++ b/solution.py
@@ -365,6 +365,17 @@
     out_ref[...] = dot_t(unit, jnp.concatenate([gath[p] for p in range(subs)], axis=0))
     for peer in peers:
         row_copy(me, peer).wait_send()
+
+
+def emit(matrix, crossed, matrix_hbm, crossed_hbm, sem):
+    copies = [
+        pltpu.make_async_copy(matrix, matrix_hbm, sem.at[0]),
+        pltpu.make_async_copy(crossed, crossed_hbm, sem.at[1]),
+    ]
+    for c in copies:
+        c.start()
+    for c in copies:
+        c.wait()
 
 
 def per_device(
@@ -437,7 +448,7 @@
             dma((subs,)),
         ],
         compiler_params=pltpu.CompilerParams(
-            collective_id=0, has_side_effects=True, vmem_limit_bytes=48 * 1024 * 1024
+            collective_id=0, has_side_effects=True, vmem_limit_bytes=40 * 1024 * 1024
         ),
     )(
         *[
@@ -455,6 +466,17 @@
             )
         ]
     )
+    group_matrix, crossed = pl.pallas_call(
+        emit,
+        out_shape=(
+            jax.ShapeDtypeStruct(group_matrix.shape, F32),
+            jax.ShapeDtypeStruct(crossed.shape, F32),
+        ),
+        in_specs=[vmem, vmem],
+        out_specs=(hbm, hbm),
+        scratch_shapes=[dma((2,))],
+        compiler_params=pltpu.CompilerParams(vmem_limit_bytes=1024 * 1024),
+    )(*[pltpu.with_memory_space_constraint(x, pltpu.VMEM) for x in (group_matrix, crossed)])
     return group_matrix[None], crossed[None, None]
 
 

time: 16.1 us -> 15.5 us (0.963)
  local copies, waits for them, and re-layouts: 1.3 us -> 0 us
  Pallas kernels: 14 us -> 14.7 us
    unnamed x2 -> x0, local copies, waits for them, and re-layouts: 1.3 us -> none
    pallas_call x0 -> x1, Pallas kernels: none -> 0.7 us  [per_device(): pl.pallas_call(emit, out_shape=(jax.ShapeDtypeStruct(group_matrix.shape,...]
where the time goes in v1:
time: 15.5 us; the launch traced here: 15.3 us
  Pallas kernels  14.7 us (95%)
  between operations  0.64 us (4%)
    pallas_call x1, Pallas kernels, per_device(): pl.pallas_call(functools.partial(kernel, subs, grps), out_shape=(pltpu.VM...  14 us
    pallas_call x1, Pallas kernels, per_device(): pl.pallas_call(emit, out_shape=(jax.ShapeDtypeStruct(group_matrix.shape,...  0.7 us

profile of v1, /device:TPU:0, one launch (start us, length us, event | category | flops | bytes accessed | tf_op | source)
XLA Modules:
  0.0 15.3 jit_solution(7233064912517932501)
XLA Ops:
  0.6 14.0 %shard_map.104 = (f32[192,192]{1,0:T(8,128)S(1)}, f32[2,48,48]{2,1,0:T(8,128)S(1)}) custom-call(bf16[32,3072]{1,0:T(8,128)(2,1)} %bitcast.16, bf16[7,32,4096]{2,1,0:T(8,128)(2,1)} %bitcast.15, bf16[4,4,4096]{2,1,0:T(4,128)(2,1)} %bitcast.17, bf16[2,2,4096]{2,1,0:T(2,128)(2,1)} %bitcast.18, s32[7,1,32]{2,1,0:T(1,128)} %bitcast.20, s32[4,256]{1,0:T(4,128)} %bitcast.19, ...), custom_call_target="tpu_custom_call" | custom-call | tf_op jit(solution)/shard_map/pallas_call | solution.py:404
  14.6 0.7 %shard_map.105 = (f32[192,192]{1,0:T(8,128)}, f32[2,48,48]{2,1,0:T(8,128)}) custom-call(f32[192,192]{1,0:T(8,128)S(1)} %get-tuple-element.6.matrix, f32[2,48,48]{2,1,0:T(8,128)S(1)} %get-tuple-element.7.crossed), custom_call_target="tpu_custom_call" | custom-call | tf_op jit(solution)/shard_map/pallas_call | solution.py:469

commit v2 on v1

--- a/solution.py
+++ b/solution.py
@@ -55,7 +55,6 @@
     pf,
     cf,
     zz,
-    zd,
     zpair,
     take_s,
     take_r,
@@ -66,6 +65,11 @@
     d_all,
     got,
     gath,
+    take_x,
+    mix_x,
+    layer_x,
+    diag_s,
+    diag_r,
     in_sem,
     lb_sem,
     ts_sem,
@@ -76,6 +80,9 @@
     fr_sem,
     rs_sem,
     rr_sem,
+    xt_sem,
+    xm_sem,
+    one_sem,
 ):
     me = lax.axis_index("sub")
     g = lax.axis_index("grp")
@@ -85,23 +92,28 @@
     step = nblk + 8
     ncb = CAP // 64
     nfb = FACE // 64
-
-    barrier = pltpu.get_barrier_semaphore()
-    for d in range(1, subs):
-        pl.semaphore_signal(
-            barrier, inc=1, device_id={"sub": lax.rem(me + d, subs)}, device_id_type=MESH
-        )
-
-    @pl.when(g > 0)
-    def _():
-        pl.semaphore_signal(barrier, inc=1, device_id={"grp": g - 1}, device_id_type=MESH)
-
-    @pl.when(g < grps - 1)
-    def _():
-        pl.semaphore_signal(barrier, inc=1, device_id={"grp": g + 1}, device_id_type=MESH)
+    last = subs - 1
+    peers = [lax.rem(me + d, subs) for d in range(subs - 1, 0, -1)]
+    sides = (g > 0).astype(jnp.int32) + (g < grps - 1).astype(jnp.int32)
+    waits = last + sides
+    lead = g == 0
 
     z_in = pltpu.make_async_copy(z_hbm, z_v, in_sem.at[0])
     z_in.start()
+    barrier = pltpu.get_barrier_semaphore()
+    below = g > 0
+    above = g < grps - 1
+    for peer in peers:
+        pl.semaphore_signal(barrier, inc=1, device_id={"sub": peer}, device_id_type=MESH)
+
+    @pl.when(below)
+    def _():
+        pl.semaphore_signal(barrier, inc=1, device_id={"grp": g - 1}, device_id_type=MESH)
+
+    @pl.when(above)
+    def _():
+        pl.semaphore_signal(barrier, inc=1, device_id={"grp": g + 1}, device_id_type=MESH)
+
     pb_in = pltpu.make_async_copy(pb_hbm, pb_v, in_sem.at[1])
     pb_in.start()
     cb_in = pltpu.make_async_copy(cb_hbm, cb_v, in_sem.at[2])
@@ -152,54 +164,6 @@
     want = jnp.where(dst < 32, dst * 2, (dst - 32) * 2 + 1)
     sel = jnp.where(src == want, 1.0, 0.0).astype(BF16)
 
-    def d_body(i, carry):
-        both = jnp.concatenate([zz[i * 2], zz[i * 2 + 1]], axis=0)
-        moved = dot(both, sel)
-        a, b = moved[:K], moved[K:]
-        zd[i * 2] = a.astype(BF16)
-        zd[i * 2 + 1] = b.astype(BF16)
-        d_all[:, pl.ds(pl.multiple_of(i * LANES, LANES), LANES)] = jnp.where(lo, a, b).astype(BF16)
-        return carry
-
-    lax.fori_loop(0, pairs, d_body, 0, unroll=8)
-
-    pb_in.wait()
-    cb_in.wait()
-    for c in small_in:
-        c.wait()
-
-    def unfold(x0, x1):
-        e = jnp.where(lo, x0, pltpu.roll(x1, HALF, 1))
-        o = jnp.where(lo, pltpu.roll(x0, HALF, 1), x1)
-        return jnp.concatenate([e, o], axis=0).astype(BF16)
-
-    def mix(x0, x1, r0, r1):
-        both = jnp.concatenate([zd[r0], zd[r1]], axis=0)[:, :HALF]
-        m = dot(both, unfold(x0, x1))
-        return jnp.where(lo, m[:K], m[K:]).astype(BF16)
-
-    def p_body(p, carry):
-        for m in range(32):
-            pf[m * 8 : m * 8 + ncb, :] = pb_v[p, :, m * LANES : (m + 1) * LANES].astype(F32)
-        parts = []
-        for c in range(0, ncb, 2):
-            x0 = pf[pl.ds(c, 32, stride=8), :]
-            x1 = pf[pl.ds(c + 1, 32, stride=8), :]
-            parts.append(mix(x0, x1, prow[p, c], prow[p, c + 1]))
-        mixed = jnp.concatenate(parts, axis=1)
-        slots = lax.broadcasted_iota(jnp.int32, (1, CAP), 1)
-        limit = jnp.where(p == me, 0, lens[0, p])
-        take_s[p] = jnp.where(slots < limit, rows_ref[pl.ds(p, 1), :], -1)
-        mix_s[p] = mixed
-        return carry
-
-    lax.fori_loop(0, subs, p_body, 0)
-    take_r[me] = jnp.full((1, CAP), -1, jnp.int32)
-    mix_r[me] = jnp.zeros((K, CAP), BF16)
-
-    waits = subs - 1 + (g > 0).astype(jnp.int32) + (g < grps - 1).astype(jnp.int32)
-    pl.semaphore_wait(barrier, waits)
-
     def take_copy(mine, theirs, peer):
         return pltpu.make_async_remote_copy(
             src_ref=take_s.at[mine],
@@ -220,11 +184,114 @@
             device_id_type=MESH,
         )
 
-    peers = [lax.rem(me + d, subs) for d in range(1, subs)]
+    def extra_take(slot):
+        return pltpu.make_async_remote_copy(
+            src_ref=take_s.at[last],
+            dst_ref=take_x.at[slot],
+            send_sem=one_sem.at[0],
+            recv_sem=xt_sem.at[slot],
+            device_id={"sub": 0},
+            device_id_type=MESH,
+        )
+
+    def extra_mix(slot):
+        return pltpu.make_async_remote_copy(
+            src_ref=mix_s.at[last],
+            dst_ref=mix_x.at[slot],
+            send_sem=one_sem.at[1],
+            recv_sem=xm_sem.at[slot],
+            device_id={"sub": 0},
+            device_id_type=MESH,
+        )
+
+    def layer_copy():
+        return pltpu.make_async_remote_copy(
+            src_ref=zpair.at[pl.ds(0, BND // LANES)],
+            dst_ref=layer_x,
+            send_sem=one_sem.at[2],
+            recv_sem=one_sem.at[3],
+            device_id={"sub": 0},
+            device_id_type=MESH,
+        )
+
+    def diag_copy():
+        return pltpu.make_async_remote_copy(
+            src_ref=diag_s,
+            dst_ref=diag_r,
+            send_sem=one_sem.at[4],
+            recv_sem=one_sem.at[5],
+            device_id={"sub": 0},
+            device_id_type=MESH,
+        )
+
+    for c in small_in:
+        c.wait()
+    slots = lax.broadcasted_iota(jnp.int32, (1, CAP), 1)
     for peer in peers:
-        take_copy(peer, me, peer).start()
-    for peer in peers:
-        mix_copy(peer, me, peer).start()
+        take_s[peer] = jnp.where(slots < lens[0, peer], rows_ref[pl.ds(peer, 1), :], -1)
+    mix_r[me] = jnp.zeros((K, CAP), BF16)
+
+    @pl.when(me == last)
+    def _():
+        pl.semaphore_wait(barrier, waits)
+
+        for p in range(last):
+            take_copy(p, last, p).start()
+
+    pb_in.wait()
+
+    def unfold(x0, x1):
+        e = jnp.where(lo, x0, pltpu.roll(x1, HALF, 1))
+        o = jnp.where(lo, pltpu.roll(x0, HALF, 1), x1)
+        return jnp.concatenate([e, o], axis=0).astype(BF16)
+
+    def mix(x0, x1, r0, r1):
+        both = dot(jnp.concatenate([zz[r0], zz[r1]], axis=0), sel).astype(BF16)[:, :HALF]
+        m = dot(both, unfold(x0, x1))
+        return jnp.where(lo, m[:K], m[K:]).astype(BF16)
+
+    for n, peer in enumerate(peers):
+        for m in range(32):
+            pf[n * 256 + m * 8 : n * 256 + m * 8 + ncb, :] = pb_v[
+                peer, :, m * LANES : (m + 1) * LANES
+            ].astype(F32)
+    for n, peer in enumerate(peers):
+        for c in range(0, ncb, 2):
+            x0 = pf[pl.ds(n * 256 + c, 32, stride=8), :]
+            x1 = pf[pl.ds(n * 256 + c + 1, 32, stride=8), :]
+            mix_s[peer, :, c * HALF : (c + 2) * HALF] = mix(
+                x0, x1, prow[peer, c], prow[peer, c + 1]
+            )
+
+    @pl.when(me == last)
+    def _():
+        for p in [*range(1, last), 0]:
+            mix_copy(p, last, p).start()
+
+        @pl.when(lead)
+        def _():
+            layer_copy().start()
+
+    @pl.when(me != last)
+    def _():
+        pl.semaphore_wait(barrier, waits)
+        sends = [last, *range(1, last), 0]
+        between = jnp.logical_and(lead, me > 0)
+
+        @pl.when(between)
+        def _():
+            extra_take(me).start()
+
+        for copy in (take_copy, mix_copy):
+            for p in sends:
+
+                @pl.when(p != me)
+                def _():
+                    copy(p, me, p).start()
+
+        @pl.when(between)
+        def _():
+            extra_mix(me).start()
 
     def face_copy(side, target):
         return pltpu.make_async_remote_copy(
@@ -236,14 +303,23 @@
             device_id_type=MESH,
         )
 
-    @pl.when(g < grps - 1)
+    @pl.when(above)
     def _():
         face_copy(0, g + 1).start()
 
-    @pl.when(g > 0)
+    @pl.when(below)
     def _():
         face_copy(1, g - 1).start()
 
+
+    def d_body(i, carry):
+        both = jnp.concatenate([zz[i * 2], zz[i * 2 + 1]], axis=0)
+        moved = dot(both, sel)
+        a, b = moved[:K], moved[K:]
+        d_all[:, pl.ds(pl.multiple_of(i * LANES, LANES), LANES)] = jnp.where(lo, a, b).astype(BF16)
+        return carry
+
+    lax.fori_loop(0, pairs, d_body, 0, unroll=8)
 
     for t in range(nnz):
         lb_in[t].wait()
@@ -281,27 +357,21 @@
         ).astype(BF16)
         return carry
 
-    lax.fori_loop(0, pairs, r_body, 0, unroll=8)
+    lax.fori_loop(0, pairs, r_body, 0, unroll=16)
     own = dot_t(a_all[...], d_all[...])
 
+    def picked(cells_of, take):
+        cells = lax.broadcasted_iota(jnp.int32, (BND, CAP), 0)
+        hot = jnp.where(cells == take, 1.0, 0.0).astype(BF16)
+        return dot(cells_of, hot).astype(BF16)
+
+    @pl.when(jnp.logical_and(lead, me == last))
+    def _():
+        diag_s[...] = own.astype(BF16)
+        diag_copy().start()
+
     layer = jnp.concatenate([zpair[h] for h in range(BND // LANES)], axis=1)
-    for peer in peers:
-        take_copy(peer, peer, peer).wait_recv()
-
-    def g_body(p, carry):
-        cells = lax.broadcasted_iota(jnp.int32, (BND, CAP), 0)
-        hot = jnp.where(cells == take_r[p], 1.0, 0.0).astype(BF16)
-        got[p] = dot(layer, hot).astype(BF16)
-        return carry
-
-    lax.fori_loop(0, subs, g_body, 0)
-
-    for peer in peers:
-        mix_copy(peer, peer, peer).wait_recv()
-    blocks = []
-    for p in range(subs):
-        blocks.append(dot_t(got[p], mix_r[p]) + jnp.where(p == me, 1.0, 0.0) * own)
-    gath[me] = jnp.concatenate(blocks, axis=1).astype(BF16)
+    got[me] = jnp.zeros((K, CAP), BF16)
 
     def row_copy(slot, peer):
         return pltpu.make_async_remote_copy(
@@ -313,8 +383,24 @@
             device_id_type=MESH,
         )
 
-    for peer in peers:
-        row_copy(me, peer).start()
+    for p in [*range(1, last), 0, last]:
+        @pl.when(p != me)
+        def _():
+            take_copy(p, p, p).wait_recv()
+            got[p] = picked(layer, take_r[p])
+            mix_copy(p, p, p).wait_recv()
+
+        block = dot_t(got[p], mix_r[p]) + jnp.where(p == me, 1.0, 0.0) * own
+        gath[me, :, p * K : (p + 1) * K] = block.astype(BF16)
+
+    for p in range(subs):
+        direct = p != me
+        if p == 0:
+            direct = jnp.logical_and(direct, jnp.logical_not(jnp.logical_and(lead, me == last)))
+
+        @pl.when(direct)
+        def _():
+            row_copy(me, p).start()
 
     @pl.when(g > 0)
     def _():
@@ -332,6 +418,7 @@
     def _():
         face[1] = jnp.zeros((K, LANES), BF16)
 
+    cb_in.wait()
     for q in range(2):
         for m in range(32):
             cf[q * 256 + m * 8 : q * 256 + m * 8 + nfb, :] = cb_v[
@@ -353,8 +440,7 @@
     for peer in peers:
         take_copy(peer, me, peer).wait_send()
         mix_copy(peer, me, peer).wait_send()
-    for peer in peers:
-        row_copy(peer, peer).wait_recv()
+
     side = subs * K
     unit = jnp.where(
         lax.broadcasted_iota(jnp.int32, (side, side), 0)
@@ -362,9 +448,57 @@
         1.0,
         0.0,
     ).astype(BF16)
-    out_ref[...] = dot_t(unit, jnp.concatenate([gath[p] for p in range(subs)], axis=0))
-    for peer in peers:
-        row_copy(me, peer).wait_send()
+
+    def put(p):
+        out_ref[:, p * K : (p + 1) * K] = dot_t(unit, gath[p])
+
+    @pl.when(jnp.logical_and(lead, me == 0))
+    def _():
+        layer_copy().wait_recv()
+        theirs = jnp.concatenate([layer_x[h] for h in range(BND // LANES)], axis=1)
+        for p in range(1, last):
+            extra_take(p).wait_recv()
+            extra_mix(p).wait_recv()
+        for p in range(last):
+            take, mixed = (take_x[p], mix_x[p]) if p else (take_s[last], mix_s[last])
+            block = dot_t(picked(theirs, take), mixed)
+            gath[last, :, p * K : (p + 1) * K] = block.astype(BF16)
+        diag_copy().wait_recv()
+        gath[last, :, last * K :] = diag_r[...]
+        put(0)
+        put(last)
+        for p in range(1, last):
+            row_copy(p, p).wait_recv()
+            put(p)
+
+    @pl.when(jnp.logical_not(jnp.logical_and(lead, me == 0)))
+    def _():
+        for p in range(subs):
+
+            @pl.when(p != me)
+            def _():
+                row_copy(p, p).wait_recv()
+
+        out_ref[...] = dot_t(unit, jnp.concatenate([gath[p] for p in range(subs)], axis=0))
+
+    @pl.when(jnp.logical_and(lead, me == last))
+    def _():
+        layer_copy().wait_send()
+        diag_copy().wait_send()
+
+    @pl.when(jnp.logical_and(lead, jnp.logical_and(me > 0, me < last)))
+    def _():
+        extra_take(me).wait_send()
+        extra_mix(me).wait_send()
+
+    for p in range(subs):
+        direct = p != me
+        if p == 0:
+            direct = jnp.logical_and(direct, jnp.logical_not(jnp.logical_and(lead, me == last)))
+
+        @pl.when(direct)
+        def _():
+            row_copy(me, p).wait_send()
 
 
 def emit(matrix, crossed, matrix_hbm, crossed_hbm, sem):
@@ -422,9 +556,8 @@
             pltpu.VMEM((K // 2 * nblk, LANES), F32),
             pltpu.VMEM((nblk * K, LANES), F32),
             pltpu.VMEM((nnz * 32 * (nblk + 8), LANES), F32),
-            pltpu.VMEM((256, LANES), F32),
+            pltpu.VMEM(((subs - 1) * 256, LANES), F32),
             pltpu.VMEM((512, LANES), F32),
-            pltpu.VMEM((nblk, K, LANES), BF16),
             pltpu.VMEM((nblk, K, LANES), BF16),
             pltpu.VMEM((nblk // 2, K, LANES), BF16),
             pltpu.VMEM((subs, 1, CAP), jnp.int32),
@@ -436,6 +569,11 @@
             pltpu.VMEM((K, nblk * HALF), BF16),
             pltpu.VMEM((subs, K, CAP), BF16),
             pltpu.VMEM((subs, K, subs * K), BF16),
+            pltpu.VMEM((subs, 1, CAP), jnp.int32),
+            pltpu.VMEM((subs, K, CAP), BF16),
+            pltpu.VMEM((BND // LANES, K, LANES), BF16),
+            pltpu.VMEM((K, K), BF16),
+            pltpu.VMEM((K, K), BF16),
             dma((8,)),
             dma((nnz,)),
             dma((subs,)),
@@ -446,6 +584,9 @@
             dma((2,)),
             dma((subs,)),
             dma((subs,)),
+            dma((subs,)),
+            dma((subs,)),
+            dma((6,)),
         ],
         compiler_params=pltpu.CompilerParams(
             collective_id=0, has_side_effects=True, vmem_limit_bytes=40 * 1024 * 1024

time: 15.5 us -> 15 us (0.968)
  Pallas kernels: 14.7 us -> 14.2 us
    pallas_call x1, Pallas kernels: 14 us -> 13.5 us  [per_device(): pl.pallas_call(functools.partial(kernel, subs, grps), out_shape=(pltpu.VM...]
where the time goes in v2:
time: 15 us; the launch traced here: 14.9 us
  Pallas kernels  14.2 us (95%)
  between operations  0.64 us (4%)
    pallas_call x1, Pallas kernels, per_device(): pl.pallas_call(functools.partial(kernel, subs, grps), out_shape=(pltpu.VM...  13.5 us
    pallas_call x1, Pallas kernels, per_device(): pl.pallas_call(emit, out_shape=(jax.ShapeDtypeStruct(group_matrix.shape,...  0.7 us

profile of v2, /device:TPU:0, one launch (start us, length us, event | category | flops | bytes accessed | tf_op | source)
XLA Modules:
  0.0 14.9 jit_solution(12816325062366173820)
XLA Ops:
  0.6 13.5 %shard_map.104 = (f32[192,192]{1,0:T(8,128)S(1)}, f32[2,48,48]{2,1,0:T(8,128)S(1)}) custom-call(bf16[32,3072]{1,0:T(8,128)(2,1)} %bitcast.16, bf16[7,32,4096]{2,1,0:T(8,128)(2,1)} %bitcast.15, bf16[4,4,4096]{2,1,0:T(4,128)(2,1)} %bitcast.17, bf16[2,2,4096]{2,1,0:T(2,128)(2,1)} %bitcast.18, s32[7,1,32]{2,1,0:T(1,128)} %bitcast.20, s32[4,256]{1,0:T(4,128)} %bitcast.19, ...), custom_call_target="tpu_custom_call" | custom-call | tf_op jit(solution)/shard_map/pallas_call | solution.py:538
  14.2 0.7 %shard_map.105 = (f32[192,192]{1,0:T(8,128)}, f32[2,48,48]{2,1,0:T(8,128)}) custom-call(f32[192,192]{1,0:T(8,128)S(1)} %get-tuple-element.6.matrix, f32[2,48,48]{2,1,0:T(8,128)S(1)} %get-tuple-element.7.crossed), custom_call_target="tpu_custom_call" | custom-call | tf_op jit(solution)/shard_map/pallas_call | solution.py:610

commit v3 on v2

--- a/solution.py
+++ b/solution.py
@@ -83,6 +83,7 @@
     xt_sem,
     xm_sem,
     one_sem,
+    ready,
 ):
     me = lax.axis_index("sub")
     g = lax.axis_index("grp")
@@ -95,16 +96,23 @@
     last = subs - 1
     peers = [lax.rem(me + d, subs) for d in range(subs - 1, 0, -1)]
     sides = (g > 0).astype(jnp.int32) + (g < grps - 1).astype(jnp.int32)
-    waits = last + sides
     lead = g == 0
+    first = jnp.logical_and(lead, me == 0)
+    waits = last + sides - first.astype(jnp.int32)
 
     z_in = pltpu.make_async_copy(z_hbm, z_v, in_sem.at[0])
     z_in.start()
     barrier = pltpu.get_barrier_semaphore()
     below = g > 0
     above = g < grps - 1
-    for peer in peers:
-        pl.semaphore_signal(barrier, inc=1, device_id={"sub": peer}, device_id_type=MESH)
+    for p in range(subs):
+        greet = p != me
+        if p == 0:
+            greet = jnp.logical_and(greet, jnp.logical_not(jnp.logical_and(lead, me == last)))
+
+        @pl.when(greet)
+        def _():
+            pl.semaphore_signal(barrier, inc=1, device_id={"sub": p}, device_id_type=MESH)
 
     @pl.when(below)
     def _():
@@ -235,6 +243,10 @@
     def _():
         pl.semaphore_wait(barrier, waits)
 
+        @pl.when(lead)
+        def _():
+            pl.semaphore_signal(ready, inc=1, device_id={"sub": 0}, device_id_type=MESH)
+
         for p in range(last):
             take_copy(p, last, p).start()
 
@@ -275,7 +287,7 @@
     @pl.when(me != last)
     def _():
         pl.semaphore_wait(barrier, waits)
-        sends = [last, *range(1, last), 0]
+        sends = [*range(1, last), last, 0]
         between = jnp.logical_and(lead, me > 0)
 
         @pl.when(between)
@@ -285,7 +297,11 @@
         for copy in (take_copy, mix_copy):
             for p in sends:
 
-                @pl.when(p != me)
+                now = p != me
+                if p == last:
+                    now = jnp.logical_and(now, jnp.logical_not(first))
+
+                @pl.when(now)
                 def _():
                     copy(p, me, p).start()
 
@@ -311,15 +327,6 @@
     def _():
         face_copy(1, g - 1).start()
 
-
-    def d_body(i, carry):
-        both = jnp.concatenate([zz[i * 2], zz[i * 2 + 1]], axis=0)
-        moved = dot(both, sel)
-        a, b = moved[:K], moved[K:]
-        d_all[:, pl.ds(pl.multiple_of(i * LANES, LANES), LANES)] = jnp.where(lo, a, b).astype(BF16)
-        return carry
-
-    lax.fori_loop(0, pairs, d_body, 0, unroll=8)
 
     for t in range(nnz):
         lb_in[t].wait()
@@ -350,9 +357,12 @@
         return dot_t(jnp.concatenate(moving, axis=1), jnp.concatenate(weights, axis=1))
 
     def r_body(i, carry):
+        at = pl.multiple_of(i * LANES, LANES)
+        moved = dot(jnp.concatenate([zz[i * 2], zz[i * 2 + 1]], axis=0), sel)
+        d_all[:, pl.ds(at, LANES)] = jnp.where(lo, moved[:K], moved[K:]).astype(BF16)
         a = own_part(i * 2)
         b = own_part(i * 2 + 1)
-        a_all[:, pl.ds(pl.multiple_of(i * LANES, LANES), LANES)] = jnp.concatenate(
+        a_all[:, pl.ds(at, LANES)] = jnp.concatenate(
             [a, b], axis=1
         ).astype(BF16)
         return carry
@@ -369,6 +379,12 @@
     def _():
         diag_s[...] = own.astype(BF16)
         diag_copy().start()
+
+    @pl.when(first)
+    def _():
+        pl.semaphore_wait(ready, 1)
+        take_copy(last, 0, last).start()
+        mix_copy(last, 0, last).start()
 
     layer = jnp.concatenate([zpair[h] for h in range(BND // LANES)], axis=1)
     got[me] = jnp.zeros((K, CAP), BF16)
@@ -452,7 +468,7 @@
     def put(p):
         out_ref[:, p * K : (p + 1) * K] = dot_t(unit, gath[p])
 
-    @pl.when(jnp.logical_and(lead, me == 0))
+    @pl.when(first)
     def _():
         layer_copy().wait_recv()
         theirs = jnp.concatenate([layer_x[h] for h in range(BND // LANES)], axis=1)
@@ -471,7 +487,7 @@
             row_copy(p, p).wait_recv()
             put(p)
 
-    @pl.when(jnp.logical_not(jnp.logical_and(lead, me == 0)))
+    @pl.when(jnp.logical_not(first))
     def _():
         for p in range(subs):
 
@@ -587,6 +603,7 @@
             dma((subs,)),
             dma((subs,)),
             dma((6,)),
+            pltpu.SemaphoreType.REGULAR,
         ],
         compiler_params=pltpu.CompilerParams(
             collective_id=0, has_side_effects=True, vmem_limit_bytes=40 * 1024 * 1024

time: 15 us -> 14.9 us (level)
    pallas_call x1, Pallas kernels: 13.5 us -> 13.4 us  [per_device(): pl.pallas_call(functools.partial(kernel, subs, grps), out_shape=(pltpu.VM...]
where the time goes in v3:
time: 14.9 us; the launch traced here: 14.7 us
  Pallas kernels  14.1 us (95%)
  between operations  0.64 us (4%)
    pallas_call x1, Pallas kernels, per_device(): pl.pallas_call(functools.partial(kernel, subs, grps), out_shape=(pltpu.VM...  13.4 us
    pallas_call x1, Pallas kernels, per_device(): pl.pallas_call(emit, out_shape=(jax.ShapeDtypeStruct(group_matrix.shape,...  0.7 us

profile of v3, /device:TPU:0, one launch (start us, length us, event | category | flops | bytes accessed | tf_op | source)
XLA Modules:
  0.0 14.7 jit_solution(4943706566433709699)
XLA Ops:
  0.6 13.4 %shard_map.104 = (f32[192,192]{1,0:T(8,128)S(1)}, f32[2,48,48]{2,1,0:T(8,128)S(1)}) custom-call(bf16[32,3072]{1,0:T(8,128)(2,1)} %bitcast.16, bf16[7,32,4096]{2,1,0:T(8,128)(2,1)} %bitcast.15, bf16[4,4,4096]{2,1,0:T(4,128)(2,1)} %bitcast.17, bf16[2,2,4096]{2,1,0:T(2,128)(2,1)} %bitcast.18, s32[7,1,32]{2,1,0:T(1,128)} %bitcast.20, s32[4,256]{1,0:T(4,128)} %bitcast.19, ...), custom_call_target="tpu_custom_call" | custom-call | tf_op jit(solution)/shard_map/pallas_call | solution.py:554
  14.0 0.7 %shard_map.105 = (f32[192,192]{1,0:T(8,128)}, f32[2,48,48]{2,1,0:T(8,128)}) custom-call(f32[192,192]{1,0:T(8,128)S(1)} %get-tuple-element.6.matrix, f32[2,48,48]{2,1,0:T(8,128)S(1)} %get-tuple-element.7.crossed), custom_call_target="tpu_custom_call" | custom-call | tf_op jit(solution)/shard_map/pallas_call | solution.py:627

commit v4 on v3

--- a/solution.py
+++ b/solution.py
@@ -253,9 +253,10 @@
     pb_in.wait()
 
     def unfold(x0, x1):
+        x0, x1 = x0.astype(BF16), x1.astype(BF16)
         e = jnp.where(lo, x0, pltpu.roll(x1, HALF, 1))
         o = jnp.where(lo, pltpu.roll(x0, HALF, 1), x1)
-        return jnp.concatenate([e, o], axis=0).astype(BF16)
+        return jnp.concatenate([e, o], axis=0)
 
     def mix(x0, x1, r0, r1):
         both = dot(jnp.concatenate([zz[r0], zz[r1]], axis=0), sel).astype(BF16)[:, :HALF]

time: 14.9 us -> 14.8 us (level)
  no operation moved by 1% of the time
where the time goes in v4:
time: 14.8 us; the launch traced here: 14.7 us
  Pallas kernels  14.1 us (95%)
  between operations  0.64 us (4%)
    pallas_call x1, Pallas kernels, per_device(): pl.pallas_call(functools.partial(kernel, subs, grps), out_shape=(pltpu.VM...  13.4 us
    pallas_call x1, Pallas kernels, per_device(): pl.pallas_call(emit, out_shape=(jax.ShapeDtypeStruct(group_matrix.shape,...  0.7 us

profile of v4, /device:TPU:0, one launch (start us, length us, event | category | flops | bytes accessed | tf_op | source)
XLA Modules:
  0.0 14.7 jit_solution(17536016523006098164)
XLA Ops:
  0.6 13.4 %shard_map.104 = (f32[192,192]{1,0:T(8,128)S(1)}, f32[2,48,48]{2,1,0:T(8,128)S(1)}) custom-call(bf16[32,3072]{1,0:T(8,128)(2,1)} %bitcast.16, bf16[7,32,4096]{2,1,0:T(8,128)(2,1)} %bitcast.15, bf16[4,4,4096]{2,1,0:T(4,128)(2,1)} %bitcast.17, bf16[2,2,4096]{2,1,0:T(2,128)(2,1)} %bitcast.18, s32[7,1,32]{2,1,0:T(1,128)} %bitcast.20, s32[4,256]{1,0:T(4,128)} %bitcast.19, ...), custom_call_target="tpu_custom_call" | custom-call | tf_op jit(solution)/shard_map/pallas_call | solution.py:555
  14.0 0.7 %shard_map.105 = (f32[192,192]{1,0:T(8,128)}, f32[2,48,48]{2,1,0:T(8,128)}) custom-call(f32[192,192]{1,0:T(8,128)S(1)} %get-tuple-element.6.matrix, f32[2,48,48]{2,1,0:T(8,128)S(1)} %get-tuple-element.7.crossed), custom_call_target="tpu_custom_call" | custom-call | tf_op jit(solution)/shard_map/pallas_call | solution.py:628

commit v5 on v4

--- a/solution.py
+++ b/solution.py
@@ -98,7 +98,8 @@
     sides = (g > 0).astype(jnp.int32) + (g < grps - 1).astype(jnp.int32)
     lead = g == 0
     first = jnp.logical_and(lead, me == 0)
-    waits = last + sides - first.astype(jnp.int32)
+    ahead = jnp.logical_and(lead, me != last)
+    waits = last + sides - ahead.astype(jnp.int32)
 
     z_in = pltpu.make_async_copy(z_hbm, z_v, in_sem.at[0])
     z_in.start()
@@ -106,11 +107,9 @@
     below = g > 0
     above = g < grps - 1
     for p in range(subs):
-        greet = p != me
-        if p == 0:
-            greet = jnp.logical_and(greet, jnp.logical_not(jnp.logical_and(lead, me == last)))
-
-        @pl.when(greet)
+        greet = jnp.logical_not(jnp.logical_and(lead, me == last))
+
+        @pl.when(jnp.logical_and(p != me, greet))
         def _():
             pl.semaphore_signal(barrier, inc=1, device_id={"sub": p}, device_id_type=MESH)
 
@@ -245,7 +244,8 @@
 
         @pl.when(lead)
         def _():
-            pl.semaphore_signal(ready, inc=1, device_id={"sub": 0}, device_id_type=MESH)
+            for p in range(last):
+                pl.semaphore_signal(ready, inc=1, device_id={"sub": p}, device_id_type=MESH)
 
         for p in range(last):
             take_copy(p, last, p).start()
@@ -288,26 +288,23 @@
     @pl.when(me != last)
     def _():
         pl.semaphore_wait(barrier, waits)
-        sends = [*range(1, last), last, 0]
+        sends = [last, *range(1, last), 0]
         between = jnp.logical_and(lead, me > 0)
+
+        for copy in (take_copy, mix_copy):
+            for p in sends:
+
+                now = p != me
+                if p == last:
+                    now = jnp.logical_and(now, jnp.logical_not(lead))
+
+                @pl.when(now)
+                def _():
+                    copy(p, me, p).start()
 
         @pl.when(between)
         def _():
             extra_take(me).start()
-
-        for copy in (take_copy, mix_copy):
-            for p in sends:
-
-                now = p != me
-                if p == last:
-                    now = jnp.logical_and(now, jnp.logical_not(first))
-
-                @pl.when(now)
-                def _():
-                    copy(p, me, p).start()
-
-        @pl.when(between)
-        def _():
             extra_mix(me).start()
 
     def face_copy(side, target):
@@ -381,11 +378,11 @@
         diag_s[...] = own.astype(BF16)
         diag_copy().start()
 
-    @pl.when(first)
+    @pl.when(ahead)
     def _():
         pl.semaphore_wait(ready, 1)
-        take_copy(last, 0, last).start()
-        mix_copy(last, 0, last).start()
+        take_copy(last, me, last).start()
+        mix_copy(last, me, last).start()
 
     layer = jnp.concatenate([zpair[h] for h in range(BND // LANES)], axis=1)
     got[me] = jnp.zeros((K, CAP), BF16)

time: 14.8 us -> 14.7 us (level)
  Pallas kernels: 14.1 us -> 13.9 us
where the time goes in v5:
time: 14.7 us; the launch traced here: 14.6 us
  Pallas kernels  13.9 us (95%)
  between operations  0.64 us (4%)
    pallas_call x1, Pallas kernels, per_device(): pl.pallas_call(functools.partial(kernel, subs, grps), out_shape=(pltpu.VM...  13.2 us
    pallas_call x1, Pallas kernels, per_device(): pl.pallas_call(emit, out_shape=(jax.ShapeDtypeStruct(group_matrix.shape,...  0.7 us

profile of v5, /device:TPU:0, one launch (start us, length us, event | category | flops | bytes accessed | tf_op | source)
XLA Modules:
  0.0 14.6 jit_solution(14543724700756104638)
XLA Ops:
  0.6 13.2 %shard_map.104 = (f32[192,192]{1,0:T(8,128)S(1)}, f32[2,48,48]{2,1,0:T(8,128)S(1)}) custom-call(bf16[32,3072]{1,0:T(8,128)(2,1)} %bitcast.16, bf16[7,32,4096]{2,1,0:T(8,128)(2,1)} %bitcast.15, bf16[4,4,4096]{2,1,0:T(4,128)(2,1)} %bitcast.17, bf16[2,2,4096]{2,1,0:T(2,128)(2,1)} %bitcast.18, s32[7,1,32]{2,1,0:T(1,128)} %bitcast.20, s32[4,256]{1,0:T(4,128)} %bitcast.19, ...), custom_call_target="tpu_custom_call" | custom-call | tf_op jit(solution)/shard_map/pallas_call | solution.py:552
  13.9 0.7 %shard_map.105 = (f32[192,192]{1,0:T(8,128)}, f32[2,48,48]{2,1,0:T(8,128)}) custom-call(f32[192,192]{1,0:T(8,128)S(1)} %get-tuple-element.6.matrix, f32[2,48,48]{2,1,0:T(8,128)S(1)} %get-tuple-element.7.crossed), custom_call_target="tpu_custom_call" | custom-call | tf_op jit(solution)/shard_map/pallas_call | solution.py:625
